TPU v7x, 32 devices: a whole 2x2x4 slice. The times are simulated.
32 devices in a mesh: grp: 2 (over y), dev: 16 (over z, x, core).
Axes of the slice: x: 2, y: 2, z: 4, core: 2. Of those that a mesh axis runs over, the one named last changes fastest.
Arguments:
- valence_orbitals: bfloat16 [4, 48, 2304], replicated, may hold values from -6 to 6
- conduction_orbitals: bfloat16 [64, 48, 2304], P('dev'), may hold values from -6 to 6
- valence_energy: float32 [4], replicated, may hold values from -6 to -1
- conduction_energy: float32 [64], P('dev'), may hold values from 0.5 to 6
- pair_index: int32 [16, 8], P('dev', 'grp'), may hold values from 0 to 15, as said below
- grid_map: int32 [24576], replicated, may hold values from 0 to 110591, as said below
Outputs:
- response: float32 [24576, 12288], P('dev', 'grp')
Inputs may be any that keep to these rules, and one draw needn't show every extreme that they name: `pair_index`: each row holds 8 distinct numbers. `grid_map`: all entries distinct.
All inputs are finite; a program needn't handle non-finite values.
Results may differ from a plain program's by a relative error of at most 0.004.
Values may be sent and summed in bfloat16 or wider, within the bound.
No kernel may reach another device: no remote copies, remote signals or barrier semaphores. Data moves between devices by JAX's collectives and lax.ppermute only.
A program may use at most 192 MiB of HBM per device.

v0:
```python
import math

import jax
import jax.numpy as jnp
from jax import lax
from jax.sharding import PartitionSpec as P

NR1 = 48
NR2 = 48
NR3 = 48
NGC = 12288


def kernel_tables(length):
    counter = jnp.arange(length, dtype=jnp.int32)
    phases = counter[:, None] * counter[None, :] % length
    angles = phases.astype(jnp.float32) * (2.0 * math.pi / length)
    return (jnp.cos(angles), jnp.sin(angles))


def highest(left, right):
    return jnp.dot(left, right, precision=lax.Precision.HIGH, preferred_element_type=jnp.float32)


def rotate_axes(values, first, second, third):
    return values.reshape(first, second, third).transpose(1, 2, 0).reshape(second, third * first)


def complex_pass(real_part, imag_part, cosines, sines):
    new_real = highest(cosines, real_part) + highest(sines, imag_part)
    new_imag = highest(cosines, imag_part) - highest(sines, real_part)
    return (new_real, new_imag)


def spectrum(density):
    cos_one, sin_one = kernel_tables(NR1)
    cos_two, sin_two = kernel_tables(NR2)
    cos_three, sin_three = kernel_tables(NR3)
    real_part = highest(cos_one, density)
    imag_part = -highest(sin_one, density)
    real_part = rotate_axes(real_part, NR1, NR2, NR3)
    imag_part = rotate_axes(imag_part, NR1, NR2, NR3)
    real_part, imag_part = complex_pass(real_part, imag_part, cos_two, sin_two)
    real_part = rotate_axes(real_part, NR2, NR3, NR1)
    imag_part = rotate_axes(imag_part, NR2, NR3, NR1)
    real_part, imag_part = complex_pass(real_part, imag_part, cos_three, sin_three)
    return (real_part.reshape(-1), imag_part.reshape(-1))


def per_device(
    valence_orbitals, conduction_orbitals, valence_energy, conduction_energy, pair_index, grid_map
):
    bands_here = conduction_orbitals.shape[0]
    plane_block = grid_map // (NR2 * NR3)
    second_index = grid_map // NR3 % NR2
    third_index = grid_map % NR3
    positions = third_index * (NR1 * NR2) + plane_block * NR2 + second_index
    inverse_root = 1.0 / math.sqrt(NR1 * NR2 * NR3)
    pair_numbers = pair_index.reshape(-1)
    local_pairs = pair_numbers.shape[0]
    valence_bands = pair_numbers // bands_here
    conduction_bands = pair_numbers % bands_here
    left = jnp.take(valence_orbitals, valence_bands, axis=0).astype(jnp.float32)
    right = jnp.take(conduction_orbitals, conduction_bands, axis=0).astype(jnp.float32)
    real_all, imag_all = jax.vmap(spectrum)(left * right)
    energy_gap = jnp.take(conduction_energy, conduction_bands) - jnp.take(
        valence_energy, valence_bands
    )
    factors = jnp.sqrt(4.0 / energy_gap) * inverse_root
    table = jnp.concatenate([real_all, imag_all], axis=0).T
    picked = jnp.take(table, positions, axis=0)
    picked = picked.T.reshape(2, local_pairs, picked.shape[0])
    scaled = picked * factors[None, :, None]
    pair_fields = scaled.transpose(1, 0, 2).astype(jnp.bfloat16)
    grouped = lax.all_gather(pair_fields, "grp", axis=0, tiled=True)
    ordered = lax.all_to_all(grouped, "dev", split_axis=2, concat_axis=0, tiled=True)
    window = pair_fields[:, :, :NGC]
    group_columns = lax.all_to_all(window, "grp", split_axis=2, concat_axis=0, tiled=True)
    every_columns = lax.all_gather(group_columns, "dev", axis=0, tiled=True)
    summed = jnp.einsum("tcr,tck->rk", ordered, every_columns, preferred_element_type=jnp.float32)
    return -summed / math.sqrt(ordered.shape[0])


def solution(mesh):
    in_specs = (P(), P("dev", None, None), P(), P("dev"), P("dev", "grp"), P())
    out_specs = P("dev", "grp")
    return jax.shard_map(
        per_device, mesh=mesh, in_specs=in_specs, out_specs=out_specs, check_vma=False
    )
```

profile of v0, /device:TPU:0, one launch (start us, length us, event | category | flops | bytes accessed | tf_op | source)
XLA Modules:
  0.0 451.9 jit_solution(1128994005979143068)
XLA Ops:
  9.1 2.4 fusion.5
  15.4 5.8 %reshape.53 = f32[4,48,48,48]{3,2,1,0:T(8,128)} reshape(f32[4,48,2304]{2,1,0:T(8,128)} %convolution_bitcast_fusion) | data formatting | bytes 3538944 | tf_op jit(solution)/shard_map/vmap()/reshape | solution.py:26
  21.2 6.4 %copy.24 = f32[4,48,48,48]{3,2,1,0:T(8,128)} copy(f32[4,48,48,48]{2,1,3,0:T(8,128)} %bitcast.109) | data formatting | bytes 3538944 | tf_op jit(solution)/shard_map/vmap()/transpose | solution.py:26
  27.6 4.2 reshape.54
  34.0 5.7 %reshape.55 = f32[4,48,48,48]{3,2,1,0:T(8,128)} reshape(f32[4,48,2304]{2,1,0:T(8,128)} %fusion.5) | data formatting | bytes 3538944 | tf_op jit(solution)/shard_map/vmap()/reshape | solution.py:26
  39.6 6.4 %copy.25 = f32[4,48,48,48]{3,2,1,0:T(8,128)} copy(f32[4,48,48,48]{2,1,3,0:T(8,128)} %bitcast.110) | data formatting | bytes 3538944 | tf_op jit(solution)/shard_map/vmap()/transpose | solution.py:26
  46.0 5.2 %reshape.56 = f32[4,48,2304]{2,1,0:T(8,128)} reshape(f32[4,48,48,48]{3,2,1,0:T(8,128)} %copy.25) | data formatting | bytes 3538944 | tf_op jit(solution)/shard_map/vmap()/reshape | solution.py:26
  51.2 2.6 fusion.23
  58.4 5.7 %reshape.59 = f32[4,48,48,48]{3,2,1,0:T(8,128)} reshape(f32[4,48,2304]{2,1,0:T(8,128)} %fusion.2) | data formatting | bytes 3538944 | tf_op jit(solution)/shard_map/vmap()/reshape | solution.py:26
  64.1 6.4 %copy.27 = f32[4,48,48,48]{3,2,1,0:T(8,128)} copy(f32[4,48,48,48]{2,1,3,0:T(8,128)} %bitcast.111) | data formatting | bytes 3538944 | tf_op jit(solution)/shard_map/vmap()/transpose | solution.py:26
  70.5 4.2 reshape.60
  76.8 5.9 %reshape.57 = f32[4,48,48,48]{3,2,1,0:T(8,128)} reshape(f32[4,48,2304]{2,1,0:T(8,128)} %fusion.1) | data formatting | bytes 3538944 | tf_op jit(solution)/shard_map/vmap()/reshape | solution.py:26
  82.7 6.4 %copy.26 = f32[4,48,48,48]{3,2,1,0:T(8,128)} copy(f32[4,48,48,48]{2,1,3,0:T(8,128)} %bitcast.112) | data formatting | bytes 3538944 | tf_op jit(solution)/shard_map/vmap()/transpose | solution.py:26
  89.0 5.2 %reshape.58 = f32[4,48,2304]{2,1,0:T(8,128)} reshape(f32[4,48,48,48]{3,2,1,0:T(8,128)} %copy.26) | data formatting | bytes 3538944 | tf_op jit(solution)/shard_map/vmap()/reshape | solution.py:26
  94.3 2.6 fusion.25
  101.2 2.5 pad_maximum_fusion
  103.7 25.7 %copy.28 = f32[8,110592]{0,1:T(8,128)} copy(f32[8,110592]{1,0:T(8,128)} %pad_maximum_fusion) | data formatting | bytes 7077888 | tf_op jit(solution)/shard_map/concatenate | solution.py:70
  129.5 99.3 %gather_fusion = f32[24576,8]{1,0:T(8,128)} fusion(f32[110592,8]{1,0:T(8,128)} %bitcast.104, s32[24576]{0:T(1024)S(1)} %broadcast_clamp_fusion), kind=kCustom, calls=%fused_computation.4 | custom fusion | bytes 1671168 | tf_op jit(solution)/shard_map/jit(_take)/gather | solution.py:71
  228.8 14.7 %select_bitcast_fusion = f32[8,24576]{0,1:T(8,128)} fusion(f32[24576,8]{1,0:T(8,128)} %gather_fusion, pred[24576]{0:T(1024)(128)(4,1)S(1)} %get-tuple-element.6), kind=kLoop, calls=%fused_computation.7 | loop fusion | flops 196608 | bytes 1597440 | tf_op jit(solution)/shard_map/jit(_take)/select_n | solution.py:71
  243.5 7.8 %copy.29 = f32[8,24576]{1,0:T(8,128)S(1)} copy(f32[8,24576]{0,1:T(8,128)} %select_bitcast_fusion) | data formatting | bytes 1572864 | tf_op jit(solution)/shard_map/jit(_take)/select_n | solution.py:71
  251.9 10.0 %copy.34 = bf16[4,2,12288]{0,1,2:T(2,128)(2,1)} copy(bf16[4,2,12288]{2,0,1:T(4,128)(2,1)S(1)} %slice.14) | data formatting | bytes 393216 | tf_op jit(solution)/shard_map/slice | solution.py:77
  261.9 14.9 %reshape.120 = bf16[2,2,24576]{2,1,0:T(2,128)(2,1)S(1)} reshape(bf16[12288,2,4]{2,1,0:T(2,128)(2,1)} %bitcast.107) | data formatting | bytes 393216
  276.8 8.9 %all_to_all.36 = bf16[2,2,24576]{2,1,0:T(2,128)(2,1)S(1)} all-to-all(bf16[2,2,24576]{2,1,0:T(2,128)(2,1)S(1)} %reshape.120), channel_id=1, replica_groups=mesh['grp'=2,'dev'=16] {'grp'}, dimensions={0} | all-to-all | bytes 393216 | tf_op jit(solution)/shard_map/all_to_all | solution.py:78
  285.7 15.1 %reshape.121 = bf16[12288,2,4]{2,1,0:T(2,128)(2,1)} reshape(bf16[2,2,24576]{2,1,0:T(2,128)(2,1)S(1)} %all_to_all.36) | data formatting | bytes 393216
  300.8 12.7 %copy.36 = bf16[2,4,2,6144]{3,1,0,2:T(4,128)(2,1)S(1)} copy(bf16[2,4,2,6144]{1,2,3,0:T(2,128)(2,1)} %bitcast.108) | data formatting | bytes 393216 | tf_op jit(solution)/shard_map/all_to_all | solution.py:78
  314.6 10.1 %all_gather.6 = bf16[8,2,24576]{2,1,0:T(2,128)(2,1)S(1)} all-gather(bf16[4,2,24576]{2,1,0:T(2,128)(2,1)S(1)} %copy.30), channel_id=1, replica_groups=mesh['grp'=2,'dev'=16] {'grp'}, dimensions={0}, use_global_device_ids=true | all-gather | bytes 1179648 | tf_op jit(solution)/shard_map/all_gather | solution.py:75
  324.8 19.4 %copy.31 = bf16[8,2,24576]{0,1,2:T(2,128)(2,1)} copy(bf16[8,2,24576]{2,1,0:T(2,128)(2,1)S(1)} %all_gather.6) | data formatting | bytes 1572864 | tf_op jit(solution)/shard_map/all_gather | solution.py:75
  344.1 15.0 %reshape.122 = bf16[16,2,12288]{2,1,0:T(2,128)(2,1)S(1)} reshape(bf16[24576,2,8]{2,1,0:T(2,128)(2,1)} %bitcast.105) | data formatting | bytes 1572864
  359.1 26.1 %all_to_all.37 = bf16[16,2,12288]{2,1,0:T(2,128)(2,1)S(1)} all-to-all(bf16[16,2,12288]{2,1,0:T(2,128)(2,1)S(1)} %reshape.122), channel_id=1, replica_groups=mesh['grp'=2,'dev'=16] {'dev'}, dimensions={0} | all-to-all | bytes 1572864 | tf_op jit(solution)/shard_map/all_to_all | solution.py:76
  385.2 15.5 %reshape.123 = bf16[24576,2,8]{2,1,0:T(2,128)(2,1)} reshape(bf16[16,2,12288]{2,1,0:T(2,128)(2,1)S(1)} %all_to_all.37) | data formatting | bytes 1572864
  400.7 26.4 %copy.40 = bf16[8,2,16,1536]{3,0,2,1:T(8,128)(2,1)S(1)} copy(bf16[8,2,16,1536]{0,1,3,2:T(2,128)(2,1)} %bitcast.106) | data formatting | bytes 1572864 | tf_op jit(solution)/shard_map/all_to_all | solution.py:76
  427.2 17.7 %fusion = f32[1536,6144]{1,0:T(8,128)} fusion(bf16[128,2,6144]{2,0,1:T(8,128)(2,1)} %all-gather.2.cloned.1.call-done, bf16[8,2,16,1536]{3,0,2,1:T(8,128)(2,1)S(1)} %copy.40), kind=kOutput, calls=%fused_computation.6 | convolution fusion | flops 4850712576 | bytes 41680896 | tf_op jit(solution)/shard_map/tcr,tck->rk/dot_general | solution.py:80
  (54 shorter events, 21.5 us)
Async XLA Ops:
  6.5 1.3 copy-start
  6.5 2.0 copy-start.8
  6.5 420.6 %all-gather.2.cloned.1.call-start = ((), (), s32[]{:S(2)}) async-start(), calls=%async_computation.2 | async-start | bytes 3342336 | tf_op jit(solution)/shard_map/all_gather | solution.py:79
  7.3 0.5 copy-start.10
  7.4 0.5 copy-start.12
  11.5 2.4 copy-start.2
  11.5 3.0 copy-start.3
  11.5 3.6 copy-start.9
  51.2 2.6 copy-start.4
  51.2 2.6 copy-start.6
  94.2 2.6 copy-start.5
  94.2 2.6 copy-start.7
  243.5 8.1 %copy-start.11 = (s32[4]{0:T(128)S(1)}, s32[4]{0:T(128)}, u32[]{:S(2)}) copy-start(s32[4]{0:T(128)} %copy-done.10) | copy-start | bytes 52
  243.5 8.1 %copy-start.13 = (s32[4]{0:T(128)S(1)}, s32[4]{0:T(128)}, u32[]{:S(2)}) copy-start(s32[4]{0:T(128)} %copy-done.12) | copy-start | bytes 52
  427.2 17.7 %copy-start.1 = (bf16[4,48,2304]{2,1,0:T(8,128)(2,1)S(1)}, bf16[4,48,2304]{2,1,0:T(8,128)(2,1)}, u32[]{:S(2)}) copy-start(bf16[4,48,2304]{2,1,0:T(8,128)(2,1)} %param.10) | copy-start | bytes 2654212
Sparse Core Ops, SparseCore 0:
  314.3 45.7 all-gather.1
where the time goes:
time: 457 us; the launch traced here: 452 us
  local copies, waits for them, and re-layouts  336 us (74%)
  blocking collectives  45.1 us (10%)
  matrix products  38.7 us (8%)
  other arithmetic  18.5 us (4%)
  between operations  13.9 us (3%)
    gather x1, local copies, waits for them, and re-layouts, per_device(): picked = jnp.take(table, positions, axis=0)  99.3 us
    unnamed x34, local copies, waits for them, and re-layouts  63.3 us
    reshape x8, local copies, waits for them, and re-layouts, rotate_axes(): values.reshape(first, second, third).transpose(1, 2, 0)  41.8 us
    all_to_all x1, local copies, waits for them, and re-layouts, per_device(): lax.all_to_all(grouped, 'dev', split_axis=2, concat_axis=0, tiled=True)  26.4 us
    all_to_all x1, blocking collectives, per_device(): lax.all_to_all(grouped, 'dev', split_axis=2, concat_axis=0, tiled=True)  26.1 us
    concatenate x1, local copies, waits for them, and re-layouts, per_device(): table = jnp.concatenate([real_all, imag_all], axis=0).T  25.7 us
    transpose x4, local copies, waits for them, and re-layouts, rotate_axes(): values.reshape(first, second, third).transpose(1, 2, 0)  25.4 us
    dot_general x10, matrix products, highest(): jnp.dot(left, right, precision=lax.Precision.HIGH, preferred_element_type...  21 us
  transfers between devices with their start and end apart: 1, of which 0 were waited for; matrix products, arithmetic and copies ran while one was open for 17% of the time, Pallas kernels for 0%

commit v1 on v0

v1 whole, which is shorter than its diff:
```python
import math

import jax
import jax.numpy as jnp
import numpy as np
from jax import lax
from jax.experimental import pallas as pl
from jax.experimental.pallas import tpu as pltpu
from jax.sharding import PartitionSpec as P

NR1 = 48
NR2 = 48
NR3 = 48
NGC = 12288
HALF = NR3 // 2 + 1
FOLD = NR2 * NR3 // 2
LANES = 128
PER_PARITY = -(-(NR2 // 2 * HALF) // LANES) * LANES
COLUMNS = 2 * PER_PARITY
TILES = COLUMNS // LANES
VMEM = 60 * 1024 * 1024


def split_bf16(values):
    high = values.astype(jnp.bfloat16)
    low = (values - high.astype(values.dtype)).astype(jnp.bfloat16)
    return high, low


def plane_tables():
    r2 = np.arange(NR2 // 2)[:, None]
    r3 = np.arange(NR3)[None, :]
    table = np.zeros((2, FOLD, PER_PARITY, 2))
    for parity in range(2):
        for half_k2 in range(NR2 // 2):
            k2 = 2 * half_k2 + parity
            for k3 in range(HALF):
                angle = 2 * np.pi * ((k2 * r2 * NR3 + k3 * r3 * NR2) % (NR2 * NR3)) / (NR2 * NR3)
                table[parity, :, half_k2 * HALF + k3, 0] = np.cos(angle).reshape(-1)
                table[parity, :, half_k2 * HALF + k3, 1] = np.sin(angle).reshape(-1)
    table = table.reshape(2, FOLD, PER_PARITY // LANES, LANES, 2).transpose(0, 2, 1, 4, 3)
    table = table.reshape(TILES, FOLD, 2 * LANES).astype(np.float32)
    high = table.astype(jnp.bfloat16)
    low = (table - high.astype(np.float32)).astype(jnp.bfloat16)
    return high, low


def first_tables():
    counter = np.arange(NR1)
    angle = 2 * np.pi * (counter[:, None] * counter[None, :] % NR1) / NR1
    cosine, sine = np.cos(angle), np.sin(angle)
    table = np.block([[cosine, -sine], [-sine, -cosine]]).astype(np.float32)
    high = table.astype(jnp.bfloat16)
    low = (table - high.astype(np.float32)).astype(jnp.bfloat16)
    return high, low


def dot32(left, right):
    return jnp.dot(left, right, preferred_element_type=jnp.float32)


def spectrum_kernel(
    pairs, bands, valence_energy, conduction_energy, valence, conduction,
    plane_high, plane_low, first_high, first_low, table, folded_high, folded_low,
):
    step = pl.program_id(0)

    @pl.when(step == 0)
    def _():
        for pair in range(pairs):
            left = valence[bands[0, pair]].astype(jnp.float32)
            right = conduction[bands[1, pair]].astype(jnp.float32)
            density = left * right
            for parity in range(2):
                if parity == 0:
                    folded = density[:, :FOLD] + density[:, FOLD:]
                else:
                    folded = density[:, :FOLD] - density[:, FOLD:]
                high, low = split_bf16(folded)
                folded_high[parity, pair * NR1 : (pair + 1) * NR1, :] = high
                folded_low[parity, pair * NR1 : (pair + 1) * NR1, :] = low

    parity = step // (TILES // 2)
    high = folded_high[parity]
    plane = dot32(high, plane_high[0]) + (
        dot32(folded_low[parity], plane_high[0]) + dot32(high, plane_low[0])
    )
    stacked = jnp.concatenate(
        [
            jnp.concatenate(
                [
                    plane[pair * NR1 : (pair + 1) * NR1, :LANES],
                    plane[pair * NR1 : (pair + 1) * NR1, LANES:],
                ],
                axis=0,
            )
            for pair in range(pairs)
        ],
        axis=1,
    )
    high, low = split_bf16(stacked)
    spectra = dot32(first_high[...], high) + (
        dot32(first_low[...], high) + dot32(first_high[...], low)
    )
    inverse_root = 1.0 / math.sqrt(NR1 * NR2 * NR3)
    for pair in range(pairs):
        gap = conduction_energy[bands[1, pair]] - valence_energy[bands[0, pair]]
        factor = jnp.sqrt(4.0 / jnp.full((8, LANES), gap, jnp.float32)) * inverse_root
        block = spectra[:, pair * LANES : (pair + 1) * LANES]
        block = block * factor[0:1, :]
        table[pair * 2 * NR1 : (pair + 1) * 2 * NR1, :] = block.astype(jnp.bfloat16)


def whole(array):
    return pl.BlockSpec(array.shape, lambda *_: (0,) * array.ndim)


def spectra_table(valence, conduction, valence_energy, conduction_energy, bands):
    pairs = bands.shape[1]
    plane_high, plane_low = plane_tables()
    first_high, first_low = first_tables()
    scalars = pl.BlockSpec(memory_space=pltpu.SMEM)
    tile = pl.BlockSpec((1, FOLD, 2 * LANES), lambda i: (i, 0, 0))

    def kernel(*refs):
        spectrum_kernel(pairs, *refs)

    return pl.pallas_call(
        kernel,
        grid=(TILES,),
        in_specs=[scalars, scalars, scalars, whole(valence), whole(conduction), tile, tile]
        + [whole(first_high), whole(first_low)],
        out_specs=pl.BlockSpec((pairs * 2 * NR1, LANES), lambda i: (0, i)),
        out_shape=jax.ShapeDtypeStruct((pairs * 2 * NR1, COLUMNS), jnp.bfloat16),
        scratch_shapes=[
            pltpu.VMEM((2, pairs * NR1, FOLD), jnp.bfloat16),
            pltpu.VMEM((2, pairs * NR1, FOLD), jnp.bfloat16),
        ],
        compiler_params=pltpu.CompilerParams(vmem_limit_bytes=VMEM),
        name="spectra",
    )(
        bands, valence_energy, conduction_energy, valence, conduction,
        jnp.asarray(plane_high), jnp.asarray(plane_low), jnp.asarray(first_high), jnp.asarray(first_low),
    )


DEPTH = 256


def plane_codes(point):
    first = point // (NR2 * NR3)
    second = point // NR3 % NR2
    third = point % NR3
    mirrored = third >= HALF
    first = jnp.where(mirrored, (NR1 - first) % NR1, first)
    second = jnp.where(mirrored, (NR2 - second) % NR2, second)
    third = jnp.where(mirrored, NR3 - third, third)
    column = second % 2 * PER_PARITY + second // 2 * HALF + third
    sign = jnp.where(mirrored, -1.0, 1.0)
    return column, first, sign


def pick_strip(point, table):
    width = point.shape[1]
    column, first, sign = plane_codes(point)
    counter = lax.broadcasted_iota(jnp.int32, (DEPTH, width), 0)
    counter = counter.astype(jnp.float32).astype(jnp.bfloat16)
    total = None
    for part in range(COLUMNS // DEPTH):
        wanted = (column - part * DEPTH).astype(jnp.float32).astype(jnp.bfloat16)
        hot = jnp.where(counter == wanted, jnp.bfloat16(1), jnp.bfloat16(0))
        term = dot32(table[:, part * DEPTH : (part + 1) * DEPTH], hot)
        total = term if total is None else total + term
    chosen = lax.broadcasted_iota(jnp.int32, (NR1, width), 0) == first
    rows = []
    for field in range(table.shape[0] // NR1):
        block = jnp.where(chosen, total[field * NR1 : (field + 1) * NR1, :], 0.0)
        row = jnp.sum(block, axis=0, keepdims=True)
        rows.append(row * sign if field % 2 else row)
    return jnp.concatenate(rows, axis=0).astype(jnp.bfloat16)


def pick(strips, table, turn, where, count):
    width = strips.shape[3]
    fields = table.shape[0] // NR1

    def kernel(_, points, table, picked):
        picked[...] = pick_strip(points[0, 0], table)

    grid_spec = pltpu.PrefetchScalarGridSpec(
        num_scalar_prefetch=1,
        grid=(count,),
        in_specs=[
            pl.BlockSpec((1, 1, 1, width), lambda i, at: (at[0] * count + i, turn, 0, 0)),
            pl.BlockSpec(memory_space=pltpu.VMEM),
        ],
        out_specs=pl.BlockSpec((fields, width), lambda i, at: (0, i)),
    )
    return pl.pallas_call(
        kernel,
        grid_spec=grid_spec,
        out_shape=jax.ShapeDtypeStruct((fields, count * width), jnp.bfloat16),
        compiler_params=pltpu.CompilerParams(vmem_limit_bytes=VMEM // 3),
        cost_estimate=pl.CostEstimate(
            flops=2 * table.size * count * width, bytes_accessed=table.size * 2, transcendentals=0
        ),
        name="pick",
    )(jnp.full((1,), where, jnp.int32), strips, table)


def response_kernel(pieces, rounds, scale, place, rows, *refs):
    out, left, right = refs[-3:]

    @pl.when(pl.program_id(0) == 0)
    def _():
        left[...] = rows[...].T

    for turn in range(rounds):
        blocks = refs[turn * len(pieces) : (turn + 1) * len(pieces)]

        @pl.when(pl.program_id(0) % rounds == turn)
        def _():
            for offsets, block in zip(pieces, blocks):
                size = block.shape[0] // len(offsets)
                for position, offset in enumerate(offsets):
                    start = pl.multiple_of(jnp.bitwise_xor(place[0], offset) * size, size)
                    right[pl.ds(start, size), :] = block[position * size : (position + 1) * size, :]

    out[...] = dot32(left[...], right[...]) * scale


def response(out, shape, row_block, place, rows, pieces, blocks, scale, width):
    depth, count = rows.shape
    rounds = len(blocks)

    def kernel(*refs):
        response_kernel(pieces, rounds, scale, *refs)

    operands = [place, rows]
    in_specs = [pl.BlockSpec(memory_space=pltpu.SMEM), whole(rows)]
    for held in blocks:
        operands += held
        in_specs += [pl.BlockSpec((block.shape[0], width), lambda i: (0, i // rounds)) for block in held]
    aliases = {}
    if out is not None:
        aliases = {len(operands): 0}
        operands.append(out)
        in_specs.append(pl.BlockSpec(memory_space=pl.ANY))
    return pl.pallas_call(
        kernel,
        grid=(shape[1] // width,),
        in_specs=in_specs,
        out_specs=pl.BlockSpec((count, width), lambda i: (row_block, i)),
        out_shape=jax.ShapeDtypeStruct(shape, jnp.float32),
        scratch_shapes=[
            pltpu.VMEM((count, depth), jnp.bfloat16),
            pltpu.VMEM((depth, width), jnp.bfloat16),
        ],
        input_output_aliases=aliases,
        compiler_params=pltpu.CompilerParams(vmem_limit_bytes=VMEM // 3),
        cost_estimate=pl.CostEstimate(
            flops=2 * depth * count * shape[1], bytes_accessed=4 * count * shape[1], transcendentals=0
        ),
        name="response",
    )(*operands)


def after(values, *others):
    return lax.optimization_barrier((values, others))[0]


def any_mesh(groups, size, table, grid_map, depth, scale):
    zero = jnp.zeros((1,), jnp.int32)
    width = 1024
    strips = grid_map.reshape(-1, 1, 1, width)
    everything = pick(strips, table, 0, 0, strips.shape[0])
    fields = everything.shape[0]
    block = lax.all_to_all(everything[:, :NGC], "grp", split_axis=1, concat_axis=0, tiled=True)
    blocks = lax.all_gather(block, "dev", axis=0, tiled=True)
    here = lax.all_to_all(everything, "dev", split_axis=1, concat_axis=0, tiled=True)
    rows = lax.all_gather(here, "grp", axis=0).reshape(groups, size, fields, -1)
    rows = rows.transpose(1, 0, 2, 3).reshape(depth, -1)
    shape = (rows.shape[1], NGC // groups)
    return response(None, shape, 0, zero, rows, [tuple(range(size))], [[blocks]], scale, 512)


def per_device(
    groups, size, valence_orbitals, conduction_orbitals, valence_energy, conduction_energy, pair_index, grid_map
):
    bands_here = conduction_orbitals.shape[0]
    own_rows = grid_map.shape[0] // size
    pair_numbers = pair_index.reshape(-1)
    fields = 2 * pair_numbers.shape[0]
    depth = groups * size * fields
    scale = -1.0 / math.sqrt(depth // 2)
    bands = jnp.stack([pair_numbers // bands_here, pair_numbers % bands_here])
    table = spectra_table(
        valence_orbitals, conduction_orbitals, valence_energy, conduction_energy, bands
    )
    if groups != 2 or size != 16:
        return any_mesh(groups, size, table, grid_map, depth, scale)

    me = lax.axis_index("grp")
    place = jnp.full((1,), lax.axis_index("dev"), jnp.int32)
    strips = grid_map.reshape(size, 2, 1, own_rows // 2)

    def across(values):
        return lax.ppermute(values, "grp", [(0, 1), (1, 0)])

    def swap(values, bit):
        return lax.ppermute(values, "dev", [(i, i ^ bit) for i in range(size)])

    def stack(*values):
        return jnp.concatenate(values, axis=0)

    def quarter(turn, where, *others):
        return pick(strips, after(table, *others), turn, where, size // 4)

    def to_rows(low, high):
        whole_round = jnp.concatenate(
            [jnp.where(me == 0, low[0], low[1]), jnp.where(me == 0, low[1], low[0]), *high], axis=1
        )
        return lax.all_to_all(whole_round, "dev", split_axis=1, concat_axis=0, tiled=True)

    def both_groups(here, there):
        both = jnp.stack([here.reshape(size, fields, -1), there.reshape(size, fields, -1)], axis=1)
        return both.reshape(depth, -1)

    other0 = quarter(0, 1 - me)
    sent0 = across(other0)
    mine0 = quarter(0, me, other0)
    own0 = stack(mine0, sent0)
    far0 = swap(own0, 8)
    other1 = quarter(1, 1 - me, own0)
    sent1 = across(other1)
    mine1 = quarter(1, me, other1)
    own1 = stack(mine1, sent1)
    near0 = stack(own0, far0)
    far1 = swap(own1, 8)
    side0, next0 = swap(near0, 2), swap(near0, 4)
    high0 = [quarter(0, 2, mine1, near0, own1)]
    high0.append(quarter(0, 3, *high0))
    near1 = stack(own1, far1)
    corner0 = swap(next0, 2)
    side1, next1 = swap(near1, 2), swap(near1, 4)
    here0 = to_rows([mine0, other0], high0)
    high1 = [quarter(1, 2, *high0, side0, next0, near1)]
    high1.append(quarter(1, 3, *high1, here0))
    there0 = across(here0)
    corner1 = swap(next1, 2)
    here1 = to_rows([mine1, other1], high1)
    there1 = across(here1)
    blocks = [[near0, side0, next0, corner0], [near1, side1, next1, corner1]]
    blocks = [held + [swap(block, 1) for block in held] for held in blocks]
    pieces = [(0, 8), (2, 10), (4, 12), (6, 14)]
    pieces += [tuple(offset + 1 for offset in piece) for piece in pieces]

    shape = (own_rows, NGC // groups)
    width = own_rows // 2
    out = response(None, shape, 0, place, both_groups(here0, there0), pieces, blocks, scale, width)
    return response(out, shape, 1, place, both_groups(here1, there1), pieces, blocks, scale, width)


def solution(mesh):
    groups, size = mesh.shape["grp"], mesh.shape["dev"]

    def body(*args):
        return per_device(groups, size, *args)

    in_specs = (P(), P("dev", None, None), P(), P("dev"), P("dev", "grp"), P())
    out_specs = P("dev", "grp")
    return jax.shard_map(body, mesh=mesh, in_specs=in_specs, out_specs=out_specs, check_vma=False)
```

time: 457 us -> 110 us (0.24)
  local copies, waits for them, and re-layouts: 336 us -> 4.2 us
  Pallas kernels: 0 us -> 64.6 us
  blocking collectives: 45.1 us -> 0 us
  matrix products: 38.7 us -> 0 us
  starting transfers between devices: 0.01 us -> 26.8 us
  other arithmetic: 18.5 us -> 4.75 us
  between operations: 13.9 us -> 0.26 us
  waiting for transfers between devices: 0.04 us -> 8.49 us
    gather x5 -> x0, local copies, waits for them, and re-layouts: 102 us -> none  [the longest x1 99.3 us: per_device(): picked = jnp.take(table, positions, axis=0)]
    pallas_call x0 -> x11, Pallas kernels: none -> 64.6 us  [the longest x8 32.6 us: pick(): pl.pallas_call(kernel, grid_spec=grid_spec, out_shape=jax.ShapeDtypeStruc...]
    unnamed x34 -> x14, local copies, waits for them, and re-layouts: 63.3 us -> 4.2 us
    reshape x9 -> x0, local copies, waits for them, and re-layouts: 42 us -> none  [the longest x8 41.8 us: rotate_axes(): values.reshape(first, second, third).transpose(1, 2, 0)]
    all_to_all x3 -> x0, local copies, waits for them, and re-layouts: 39.8 us -> none  [the longest x1 26.4 us: per_device(): lax.all_to_all(grouped, 'dev', split_axis=2, concat_axis=0, tiled=True)]
    dot_general x11 -> x0, matrix products: 38.7 us -> none  [the longest x10 21 us: highest(): jnp.dot(left, right, precision=lax.Precision.HIGH, preferred_element_type...]
    all_to_all x2 -> x0, blocking collectives: 34.9 us -> none  [the longest x1 26.1 us: per_device(): lax.all_to_all(grouped, 'dev', split_axis=2, concat_axis=0, tiled=True)]
    concatenate x1 -> x0, local copies, waits for them, and re-layouts: 25.7 us -> none  [per_device(): table = jnp.concatenate([real_all, imag_all], axis=0).T]
  transfers between devices with their start and end apart: 1 -> 22, of which waited for: 0 -> 4; matrix products, arithmetic and copies ran while one was open for 17% -> 2% of each run, Pallas kernels for 0% -> 31%
where the time goes in v1:
time: 110 us; the launch traced here: 109 us
  Pallas kernels  64.6 us (59%)
  starting transfers between devices  26.8 us (24%)
  waiting for transfers between devices  8.49 us (8%)
  other arithmetic  4.75 us (4%)
  local copies, waits for them, and re-layouts  4.2 us (4%)
    pallas_call x8, Pallas kernels, pick(): pl.pallas_call(kernel, grid_spec=grid_spec, out_shape=jax.ShapeDtypeStruc...  32.6 us
    pallas_call x2, Pallas kernels, response(): pl.pallas_call(kernel, grid=(shape[1] // width,), in_specs=in_specs, out_...  18.2 us
    pallas_call x1, Pallas kernels, spectra_table(): pl.pallas_call(kernel, grid=(TILES,), in_specs=[scalars, scalars, scalars...  13.8 us
    ppermute x16, starting transfers between devices, swap(): return lax.ppermute(values, 'dev', [(i, i ^ bit) for i in range(size)])  13.6 us
    all_to_all x2, starting transfers between devices, to_rows(): lax.all_to_all(whole_round, 'dev', split_axis=1, concat_axis=0, tiled=True)  8.13 us
    all_to_all x2, waiting for transfers between devices, to_rows(): lax.all_to_all(whole_round, 'dev', split_axis=1, concat_axis=0, tiled=True)  7.62 us
    ppermute x4, starting transfers between devices, across(): return lax.ppermute(values, 'grp', [(0, 1), (1, 0)])  5.15 us
    unnamed x14, local copies, waits for them, and re-layouts  4.2 us
  transfers between devices with their start and end apart: 22, of which 4 were waited for; matrix products, arithmetic and copies ran while one was open for 2% of the time, Pallas kernels for 31%

profile of v1, /device:TPU:0, one launch (start us, length us, event | category | flops | bytes accessed | tf_op | source)
XLA Modules:
  0.0 109.2 jit_solution(12847145799044190313)
XLA Ops:
  0.0 0.7 and_select_fusion.1
  1.3 13.8 %spectra.1.table = bf16[384,1280]{1,0:T(8,128)(2,1)} custom-call(s32[2,4]{1,0:T(2,128)} %pad_add_fusion.refs_0_, f32[4]{0:T(128)} %refs_1_.1, f32[4]{0:T(128)} %refs_2_.1, bf16[4,48,2304]{2,1,0:T(8,128)(2,1)} %refs_3_.1, bf16[4,48,2304]{2,1,0:T(8,128)(2,1)} %refs_4_.1, bf16[10,1152,256]{2,1,0:T(8,128)(2,1)} %constant.51.clone.refs_5_, ...), custom_call_target="tpu_custom_call" | custom-call | tf_op jit(solution)/shard_map/spectra/pallas_call | solution.py:128
  15.1 1.2 %copy-done = bf16[384,1280]{1,0:T(8,128)(2,1)S(1)} copy-done((bf16[384,1280]{1,0:T(8,128)(2,1)S(1)}, bf16[384,1280]{1,0:T(8,128)(2,1)}, u32[]{:S(2)}) %copy-start) | copy-done | bytes 983064
  16.3 0.9 copy-done.3
  17.2 4.0 %pick.8 = bf16[8,3072]{1,0:T(8,128)(2,1)S(1)} custom-call(s32[1]{0:T(128)} %bitcast.3._, s32[16,2,1,768]{3,2,1,0:T(1,128)S(1)} %bitcast.22, bf16[384,1280]{1,0:T(8,128)(2,1)S(1)} %copy-done), custom_call_target="tpu_custom_call" | custom-call | flops 3019898880 | bytes 983040 | tf_op jit(solution)/shard_map/pick/pallas_call | solution.py:199
  21.3 3.0 %collective-permute-start = (bf16[8,3072]{1,0:T(8,128)(2,1)S(1)}, bf16[8,3072]{1,0:T(8,128)(2,1)S(1)}, u32[]{:S(2)}, u32[]{:S(2)}) collective-permute-start(bf16[8,3072]{1,0:T(8,128)(2,1)S(1)} %pick.8), channel_id=1, source_target_pairs={{0,16},{16,0},{1,17},{17,1},{2,18},{18,2},{3,19},{19,3},{4,20},{20... | collective-permute-start | bytes 147464 | tf_op jit(solution)/shard_map/ppermute | solution.py:308
  24.3 1.2 %copy-done.1 = bf16[384,1280]{1,0:T(8,128)(2,1)S(1)} copy-done((bf16[384,1280]{1,0:T(8,128)(2,1)S(1)}, bf16[384,1280]{1,0:T(8,128)(2,1)}, u32[]{:S(2)}) %copy-start.1) | copy-done | bytes 983064
  25.5 0.9 copy-done.4
  26.4 4.1 %pick.9 = bf16[8,3072]{1,0:T(8,128)(2,1)S(1)} custom-call(s32[1]{0:T(128)} %bitcast.1._, s32[16,2,1,768]{3,2,1,0:T(1,128)S(1)} %bitcast.23, bf16[384,1280]{1,0:T(8,128)(2,1)S(1)} %copy-done.1), custom_call_target="tpu_custom_call" | custom-call | flops 3019898880 | bytes 983040 | tf_op jit(solution)/shard_map/pick/pallas_call | solution.py:199
  30.5 4.1 %pick.10 = bf16[8,3072]{1,0:T(8,128)(2,1)S(1)} custom-call(s32[1]{0:T(128)} %bitcast.3._, s32[16,2,1,768]{3,2,1,0:T(1,128)S(1)} %bitcast.24, bf16[384,1280]{1,0:T(8,128)(2,1)S(1)} %copy-done.1), custom_call_target="tpu_custom_call" | custom-call | flops 3019898880 | bytes 983040 | tf_op jit(solution)/shard_map/pick/pallas_call | solution.py:199
  34.7 3.1 %collective-permute-start.1 = (bf16[16,3072]{1,0:T(8,128)(2,1)S(1)}, bf16[16,3072]{1,0:T(8,128)(2,1)S(1)}, u32[]{:S(2)}, u32[]{:S(2)}) collective-permute-start(bf16[16,3072]{1,0:T(8,128)(2,1)S(1)} %pad_maximum_fusion.6), channel_id=1, source_target_pairs={{0,8},{1,9},{2,10},{3,11},{4,12},{5,13},{6,14},{7,15},{8,0},{9,1},... | collective-permute-start | bytes 294920 | tf_op jit(solution)/shard_map/ppermute | solution.py:311
  37.8 4.1 %pick.11 = bf16[8,3072]{1,0:T(8,128)(2,1)S(1)} custom-call(s32[1]{0:T(128)} %bitcast.1._, s32[16,2,1,768]{3,2,1,0:T(1,128)S(1)} %bitcast.25, bf16[384,1280]{1,0:T(8,128)(2,1)S(1)} %copy-done.1), custom_call_target="tpu_custom_call" | custom-call | flops 3019898880 | bytes 983040 | tf_op jit(solution)/shard_map/pick/pallas_call | solution.py:199
  42.2 1.8 %collective-permute-start.4 = (bf16[32,3072]{1,0:T(8,128)(2,1)S(1)}, bf16[32,3072]{1,0:T(8,128)(2,1)S(1)}, u32[]{:S(2)}, u32[]{:S(2)}) collective-permute-start(bf16[32,3072]{1,0:T(8,128)(2,1)S(1)} %pad_maximum_fusion.2.refs_2_), channel_id=1, source_target_pairs={{0,4},{1,5},{2,6},{3,7},{4,0},{5,1},{6,2},{7,3},{8,12},{9,13},{10,... | collective-permute-start | bytes 589832 | tf_op jit(solution)/shard_map/ppermute | solution.py:311
  44.1 1.5 %collective-permute-start.3 = (bf16[32,3072]{1,0:T(8,128)(2,1)S(1)}, bf16[32,3072]{1,0:T(8,128)(2,1)S(1)}, u32[]{:S(2)}, u32[]{:S(2)}) collective-permute-start(bf16[32,3072]{1,0:T(8,128)(2,1)S(1)} %pad_maximum_fusion.2.refs_2_), channel_id=1, source_target_pairs={{0,2},{1,3},{2,0},{3,1},{4,6},{5,7},{6,4},{7,5},{8,10},{9,11},{10,... | collective-permute-start | bytes 589832 | tf_op jit(solution)/shard_map/ppermute | solution.py:311
  45.6 4.1 %pick.12 = bf16[8,3072]{1,0:T(8,128)(2,1)S(1)} custom-call(s32[1]{0:T(128)} %constant.49.clone.1._, s32[16,2,1,768]{3,2,1,0:T(1,128)S(1)} %bitcast.26, bf16[384,1280]{1,0:T(8,128)(2,1)S(1)} %copy-done.1), custom_call_target="tpu_custom_call" | custom-call | flops 3019898880 | bytes 983040 | tf_op jit(solution)/shard_map/pick/pallas_call | solution.py:199
  49.6 4.1 %pick.13 = bf16[8,3072]{1,0:T(8,128)(2,1)S(1)} custom-call(s32[1]{0:T(128)} %constant.50.clone.1._, s32[16,2,1,768]{3,2,1,0:T(1,128)S(1)} %bitcast.27, bf16[384,1280]{1,0:T(8,128)(2,1)S(1)} %copy-done.1), custom_call_target="tpu_custom_call" | custom-call | flops 3019898880 | bytes 983040 | tf_op jit(solution)/shard_map/pick/pallas_call | solution.py:199
  54.4 4.0 %all-to-all-start = ((bf16[8,16,768]{2,0,1:T(8,128)(2,1)}), bf16[8,16,768]{2,0,1:T(8,128)(2,1)S(1)}, u32[]{:S(2)}, u32[]{:S(2)}) async-start(bf16[8,16,768]{2,0,1:T(8,128)(2,1)} %bitcast.4), calls=%async_computation | async-start | bytes 393216 | tf_op jit(solution)/shard_map/all_to_all | solution.py:323
  58.9 1.7 %collective-permute-start.13 = (bf16[32,3072]{1,0:T(8,128)(2,1)S(1)}, bf16[32,3072]{1,0:T(8,128)(2,1)S(1)}, u32[]{:S(2)}, u32[]{:S(2)}) collective-permute-start(bf16[32,3072]{1,0:T(8,128)(2,1)S(1)} %pad_maximum_fusion.3.refs_10_), channel_id=1, source_target_pairs={{0,4},{1,5},{2,6},{3,7},{4,0},{5,1},{6,2},{7,3},{8,12},{9,13},{10,... | collective-permute-start | bytes 589832 | tf_op jit(solution)/shard_map/ppermute | solution.py:311
  60.6 1.5 %collective-permute-start.12 = (bf16[32,3072]{1,0:T(8,128)(2,1)S(1)}, bf16[32,3072]{1,0:T(8,128)(2,1)S(1)}, u32[]{:S(2)}, u32[]{:S(2)}) collective-permute-start(bf16[32,3072]{1,0:T(8,128)(2,1)S(1)} %pad_maximum_fusion.3.refs_10_), channel_id=1, source_target_pairs={{0,2},{1,3},{2,0},{3,1},{4,6},{5,7},{6,4},{7,5},{8,10},{9,11},{10,... | collective-permute-start | bytes 589832 | tf_op jit(solution)/shard_map/ppermute | solution.py:311
  62.1 4.1 %pick.14 = bf16[8,3072]{1,0:T(8,128)(2,1)S(1)} custom-call(s32[1]{0:T(128)} %constant.49.clone.1._, s32[16,2,1,768]{3,2,1,0:T(1,128)S(1)} %bitcast.28, bf16[384,1280]{1,0:T(8,128)(2,1)S(1)} %copy-done.2), custom_call_target="tpu_custom_call" | custom-call | flops 3019898880 | bytes 983040 | tf_op jit(solution)/shard_map/pick/pallas_call | solution.py:199
  66.2 1.7 %all-to-all-done = bf16[8,16,768]{2,0,1:T(8,128)(2,1)S(1)} async-done(((bf16[8,16,768]{2,0,1:T(8,128)(2,1)}), bf16[8,16,768]{2,0,1:T(8,128)(2,1)S(1)}, u32[]{:S(2)}, u32[]{:S(2)}) %all-to-all-start) | async-done | bytes 196640 | tf_op jit(solution)/shard_map/all_to_all | solution.py:323
  67.9 4.0 %pick.15 = bf16[8,3072]{1,0:T(8,128)(2,1)S(1)} custom-call(s32[1]{0:T(128)} %constant.50.clone.1._, s32[16,2,1,768]{3,2,1,0:T(1,128)S(1)} %bitcast.29, bf16[384,1280]{1,0:T(8,128)(2,1)S(1)} %copy-done.2), custom_call_target="tpu_custom_call" | custom-call | flops 3019898880 | bytes 983040 | tf_op jit(solution)/shard_map/pick/pallas_call | solution.py:199
  72.0 2.0 %collective-permute-start.14 = (bf16[32,3072]{1,0:T(8,128)(2,1)S(1)}, bf16[32,3072]{1,0:T(8,128)(2,1)S(1)}, u32[]{:S(2)}, u32[]{:S(2)}) collective-permute-start(bf16[32,3072]{1,0:T(8,128)(2,1)S(1)} %collective-permute-done.13.refs_12_), channel_id=1, source_target_pairs={{0,2},{1,3},{2,0},{3,1},{4,6},{5,7},{6,4},{7,5},{8,10},{9,11},{10,... | collective-permute-start | bytes 589832 | tf_op jit(solution)/shard_map/ppermute | solution.py:311
  74.0 1.5 %collective-permute-start.19 = (bf16[128,768]{1,0:T(8,128)(2,1)S(1)}, bf16[128,768]{1,0:T(8,128)(2,1)}, u32[]{:S(2)}, u32[]{:S(2)}) collective-permute-start(bf16[128,768]{1,0:T(8,128)(2,1)S(1)} %bitcast.30), channel_id=1, source_target_pairs={{0,16},{16,0},{1,17},{17,1},{2,18},{18,2},{3,19},{19,3},{4,20},{20... | collective-permute-start | bytes 589832 | tf_op jit(solution)/shard_map/ppermute | solution.py:308
  75.6 0.7 pad_maximum_fusion.5
  76.2 4.2 %all-to-all-start.1 = ((bf16[8,16,768]{2,0,1:T(8,128)(2,1)}), bf16[8,16,768]{2,0,1:T(8,128)(2,1)}, u32[]{:S(2)}, u32[]{:S(2)}) async-start(bf16[8,16,768]{2,0,1:T(8,128)(2,1)} %bitcast.7), calls=%async_computation.1 | async-start | bytes 393216 | tf_op jit(solution)/shard_map/all_to_all | solution.py:323
  81.3 0.7 collective-permute-done.14.refs_13_
  82.5 1.1 pad_maximum_fusion.1
  83.5 5.9 %all-to-all-done.1 = bf16[8,16,768]{2,0,1:T(8,128)(2,1)} async-done(((bf16[8,16,768]{2,0,1:T(8,128)(2,1)}), bf16[8,16,768]{2,0,1:T(8,128)(2,1)}, u32[]{:S(2)}, u32[]{:S(2)}) %all-to-all-start.1) | async-done | bytes 196640 | tf_op jit(solution)/shard_map/all_to_all | solution.py:323
  90.0 9.1 %response.2.refs_18_ = f32[1536,6144]{1,0:T(8,128)} custom-call(s32[1]{0:T(128)} %bitcast.refs_0_, bf16[256,768]{1,0:T(8,128)(2,1)S(1)} %bitcast.20, bf16[32,3072]{1,0:T(8,128)(2,1)S(1)} %pad_maximum_fusion.2.refs_2_, bf16[32,3072]{1,0:T(8,128)(2,1)S(1)} %collective-permute-done.3.refs_3_, bf16[32,3072]{1,0:T(8,128)(2,1)S(1)} %collective-permute-done.4.refs_4_, ...), custom_call_target="tpu_custom_call" | custom-call | flops 2415919104 | bytes 18874368 | tf_op jit(solution)/shard_map/response/pallas_call | solution.py:249
  99.1 1.0 pad_maximum_fusion
  100.0 9.1 %response.3 = f32[1536,6144]{1,0:T(8,128)} custom-call(s32[1]{0:T(128)} %bitcast.refs_0_, bf16[256,768]{1,0:T(8,128)(2,1)S(1)} %bitcast.21, bf16[32,3072]{1,0:T(8,128)(2,1)S(1)} %pad_maximum_fusion.2.refs_2_, bf16[32,3072]{1,0:T(8,128)(2,1)S(1)} %collective-permute-done.3.refs_3_, ...), custom_call_target="tpu_custom_call", output_to_operand_aliasing={{}: (18, {})} | custom-call | flops 2415919104 | bytes 18874368 | tf_op jit(solution)/shard_map/response/pallas_call | solution.py:249
  (49 shorter events, 4.1 us)
Async XLA Ops:
  0.0 49.6 %copy-start.5 = (s32[24576]{0:T(1024)S(1)}, s32[24576]{0:T(1024)}, u32[]{:S(2)}) copy-start(s32[24576]{0:T(1024)} %param.15) | copy-start | bytes 294916
  15.1 1.2 %copy-start = (bf16[384,1280]{1,0:T(8,128)(2,1)S(1)}, bf16[384,1280]{1,0:T(8,128)(2,1)}, u32[]{:S(2)}) copy-start(bf16[384,1280]{1,0:T(8,128)(2,1)} %spectra.1.table) | copy-start | bytes 2949124
  16.3 0.9 copy-start.3
  17.2 44.8 %copy-start.2 = (bf16[384,1280]{1,0:T(8,128)(2,1)S(1)}, bf16[384,1280]{1,0:T(8,128)(2,1)}, u32[]{:S(2)}) copy-start(bf16[384,1280]{1,0:T(8,128)(2,1)} %spectra.1.table) | copy-start | bytes 2949124
  21.3 9.2 %collective-permute-start = (bf16[8,3072]{1,0:T(8,128)(2,1)S(1)}, bf16[8,3072]{1,0:T(8,128)(2,1)S(1)}, u32[]{:S(2)}, u32[]{:S(2)}) collective-permute-start(bf16[8,3072]{1,0:T(8,128)(2,1)S(1)} %pick.8), channel_id=1, source_target_pairs={{0,16},{16,0},{1,17},{17,1},{2,18},{18,2},{3,19},{19,3},{4,20},{20... | collective-permute-start | bytes 147464 | tf_op jit(solution)/shard_map/ppermute | solution.py:308
  24.3 1.2 %copy-start.1 = (bf16[384,1280]{1,0:T(8,128)(2,1)S(1)}, bf16[384,1280]{1,0:T(8,128)(2,1)}, u32[]{:S(2)}) copy-start(bf16[384,1280]{1,0:T(8,128)(2,1)} %spectra.1.table) | copy-start | bytes 2949124
  25.5 0.9 copy-start.4
  34.6 7.3 %collective-permute-start.2 = (bf16[8,3072]{1,0:T(8,128)(2,1)S(1)}, bf16[8,3072]{1,0:T(8,128)(2,1)S(1)}, u32[]{:S(2)}, u32[]{:S(2)}) collective-permute-start(bf16[8,3072]{1,0:T(8,128)(2,1)S(1)} %pick.10), channel_id=1, source_target_pairs={{0,16},{16,0},{1,17},{17,1},{2,18},{18,2},{3,19},{19,3},{4,20},{20... | collective-permute-start | bytes 147464 | tf_op jit(solution)/shard_map/ppermute | solution.py:308
  34.7 7.4 %collective-permute-start.1 = (bf16[16,3072]{1,0:T(8,128)(2,1)S(1)}, bf16[16,3072]{1,0:T(8,128)(2,1)S(1)}, u32[]{:S(2)}, u32[]{:S(2)}) collective-permute-start(bf16[16,3072]{1,0:T(8,128)(2,1)S(1)} %pad_maximum_fusion.6), channel_id=1, source_target_pairs={{0,8},{1,9},{2,10},{3,11},{4,12},{5,13},{6,14},{7,15},{8,0},{9,1},... | collective-permute-start | bytes 294920 | tf_op jit(solution)/shard_map/ppermute | solution.py:311
  41.9 16.5 %collective-permute-start.5 = (bf16[16,3072]{1,0:T(8,128)(2,1)S(1)}, bf16[16,3072]{1,0:T(8,128)(2,1)S(1)}, u32[]{:S(2)}, u32[]{:S(2)}) collective-permute-start(bf16[16,3072]{1,0:T(8,128)(2,1)S(1)} %pad_maximum_fusion.7), channel_id=1, source_target_pairs={{0,8},{1,9},{2,10},{3,11},{4,12},{5,13},{6,14},{7,15},{8,0},{9,1},... | collective-permute-start | bytes 294920 | tf_op jit(solution)/shard_map/ppermute | solution.py:311
  42.2 29.8 %collective-permute-start.8 = (bf16[32,3072]{1,0:T(8,128)(2,1)S(1)}, bf16[32,3072]{1,0:T(8,128)(2,1)S(1)}, u32[]{:S(2)}, u32[]{:S(2)}) collective-permute-start(bf16[32,3072]{1,0:T(8,128)(2,1)S(1)} %pad_maximum_fusion.2.refs_2_), channel_id=1, source_target_pairs={{0,1},{1,0},{2,3},{3,2},{4,5},{5,4},{6,7},{7,6},{8,9},{9,8},{10,11... | collective-permute-start | bytes 589832 | tf_op jit(solution)/shard_map/ppermute | solution.py:311
  42.2 18.3 %collective-permute-start.4 = (bf16[32,3072]{1,0:T(8,128)(2,1)S(1)}, bf16[32,3072]{1,0:T(8,128)(2,1)S(1)}, u32[]{:S(2)}, u32[]{:S(2)}) collective-permute-start(bf16[32,3072]{1,0:T(8,128)(2,1)S(1)} %pad_maximum_fusion.2.refs_2_), channel_id=1, source_target_pairs={{0,4},{1,5},{2,6},{3,7},{4,0},{5,1},{6,2},{7,3},{8,12},{9,13},{10,... | collective-permute-start | bytes 589832 | tf_op jit(solution)/shard_map/ppermute | solution.py:311
  44.1 18.0 %collective-permute-start.3 = (bf16[32,3072]{1,0:T(8,128)(2,1)S(1)}, bf16[32,3072]{1,0:T(8,128)(2,1)S(1)}, u32[]{:S(2)}, u32[]{:S(2)}) collective-permute-start(bf16[32,3072]{1,0:T(8,128)(2,1)S(1)} %pad_maximum_fusion.2.refs_2_), channel_id=1, source_target_pairs={{0,2},{1,3},{2,0},{3,1},{4,6},{5,7},{6,4},{7,5},{8,10},{9,11},{10,... | collective-permute-start | bytes 589832 | tf_op jit(solution)/shard_map/ppermute | solution.py:311
  54.4 13.4 %all-to-all-start = ((bf16[8,16,768]{2,0,1:T(8,128)(2,1)}), bf16[8,16,768]{2,0,1:T(8,128)(2,1)S(1)}, u32[]{:S(2)}, u32[]{:S(2)}) async-start(bf16[8,16,768]{2,0,1:T(8,128)(2,1)} %bitcast.4), calls=%async_computation | async-start | bytes 393216 | tf_op jit(solution)/shard_map/all_to_all | solution.py:323
  58.4 15.6 %collective-permute-start.15 = (bf16[32,3072]{1,0:T(8,128)(2,1)S(1)}, bf16[32,3072]{1,0:T(8,128)(2,1)S(1)}, u32[]{:S(2)}, u32[]{:S(2)}) collective-permute-start(bf16[32,3072]{1,0:T(8,128)(2,1)S(1)} %pad_maximum_fusion.3.refs_10_), channel_id=1, source_target_pairs={{0,1},{1,0},{2,3},{3,2},{4,5},{5,4},{6,7},{7,6},{8,9},{9,8},{10,11... | collective-permute-start | bytes 589832 | tf_op jit(solution)/shard_map/ppermute | solution.py:311
  58.9 13.1 %collective-permute-start.13 = (bf16[32,3072]{1,0:T(8,128)(2,1)S(1)}, bf16[32,3072]{1,0:T(8,128)(2,1)S(1)}, u32[]{:S(2)}, u32[]{:S(2)}) collective-permute-start(bf16[32,3072]{1,0:T(8,128)(2,1)S(1)} %pad_maximum_fusion.3.refs_10_), channel_id=1, source_target_pairs={{0,4},{1,5},{2,6},{3,7},{4,0},{5,1},{6,2},{7,3},{8,12},{9,13},{10,... | collective-permute-start | bytes 589832 | tf_op jit(solution)/shard_map/ppermute | solution.py:311
  60.6 19.9 %collective-permute-start.12 = (bf16[32,3072]{1,0:T(8,128)(2,1)S(1)}, bf16[32,3072]{1,0:T(8,128)(2,1)S(1)}, u32[]{:S(2)}, u32[]{:S(2)}) collective-permute-start(bf16[32,3072]{1,0:T(8,128)(2,1)S(1)} %pad_maximum_fusion.3.refs_10_), channel_id=1, source_target_pairs={{0,2},{1,3},{2,0},{3,1},{4,6},{5,7},{6,4},{7,5},{8,10},{9,11},{10,... | collective-permute-start | bytes 589832 | tf_op jit(solution)/shard_map/ppermute | solution.py:311
  62.0 18.7 %collective-permute-start.10 = (bf16[32,3072]{1,0:T(8,128)(2,1)S(1)}, bf16[32,3072]{1,0:T(8,128)(2,1)S(1)}, u32[]{:S(2)}, u32[]{:S(2)}) collective-permute-start(bf16[32,3072]{1,0:T(8,128)(2,1)S(1)} %collective-permute-done.4.refs_4_), channel_id=1, source_target_pairs={{0,1},{1,0},{2,3},{3,2},{4,5},{5,4},{6,7},{7,6},{8,9},{9,8},{10,11... | collective-permute-start | bytes 589832 | tf_op jit(solution)/shard_map/ppermute | solution.py:311
  67.9 14.1 %copy-start.6 = (bf16[8,16,768]{2,0,1:T(8,128)(2,1)}, bf16[8,16,768]{2,0,1:T(8,128)(2,1)S(1)}, u32[]{:S(2)}) copy-start(bf16[8,16,768]{2,0,1:T(8,128)(2,1)S(1)} %all-to-all-done) | copy-start | bytes 589828
  71.9 9.1 %collective-permute-start.7 = (bf16[32,3072]{1,0:T(8,128)(2,1)S(1)}, bf16[32,3072]{1,0:T(8,128)(2,1)S(1)}, u32[]{:S(2)}, u32[]{:S(2)}) collective-permute-start(bf16[32,3072]{1,0:T(8,128)(2,1)S(1)} %collective-permute-done.4.refs_4_), channel_id=1, source_target_pairs={{0,2},{1,3},{2,0},{3,1},{4,6},{5,7},{6,4},{7,5},{8,10},{9,11},{10,... | collective-permute-start | bytes 589832 | tf_op jit(solution)/shard_map/ppermute | solution.py:311
  72.0 9.9 %collective-permute-start.14 = (bf16[32,3072]{1,0:T(8,128)(2,1)S(1)}, bf16[32,3072]{1,0:T(8,128)(2,1)S(1)}, u32[]{:S(2)}, u32[]{:S(2)}) collective-permute-start(bf16[32,3072]{1,0:T(8,128)(2,1)S(1)} %collective-permute-done.13.refs_12_), channel_id=1, source_target_pairs={{0,2},{1,3},{2,0},{3,1},{4,6},{5,7},{6,4},{7,5},{8,10},{9,11},{10,... | collective-permute-start | bytes 589832 | tf_op jit(solution)/shard_map/ppermute | solution.py:311
  74.0 7.9 %collective-permute-start.19 = (bf16[128,768]{1,0:T(8,128)(2,1)S(1)}, bf16[128,768]{1,0:T(8,128)(2,1)}, u32[]{:S(2)}, u32[]{:S(2)}) collective-permute-start(bf16[128,768]{1,0:T(8,128)(2,1)S(1)} %bitcast.30), channel_id=1, source_target_pairs={{0,16},{16,0},{1,17},{17,1},{2,18},{18,2},{3,19},{19,3},{4,20},{20... | collective-permute-start | bytes 589832 | tf_op jit(solution)/shard_map/ppermute | solution.py:308
  76.2 13.2 %all-to-all-start.1 = ((bf16[8,16,768]{2,0,1:T(8,128)(2,1)}), bf16[8,16,768]{2,0,1:T(8,128)(2,1)}, u32[]{:S(2)}, u32[]{:S(2)}) async-start(bf16[8,16,768]{2,0,1:T(8,128)(2,1)} %bitcast.7), calls=%async_computation.1 | async-start | bytes 393216 | tf_op jit(solution)/shard_map/all_to_all | solution.py:323
  80.4 3.1 %collective-permute-start.9 = (bf16[32,3072]{1,0:T(8,128)(2,1)S(1)}, bf16[32,3072]{1,0:T(8,128)(2,1)S(1)}, u32[]{:S(2)}, u32[]{:S(2)}) collective-permute-start(bf16[32,3072]{1,0:T(8,128)(2,1)S(1)} %collective-permute-done.3.refs_3_), channel_id=1, source_target_pairs={{0,1},{1,0},{2,3},{3,2},{4,5},{5,4},{6,7},{7,6},{8,9},{9,8},{10,11... | collective-permute-start | bytes 589832 | tf_op jit(solution)/shard_map/ppermute | solution.py:311
  80.7 9.2 %collective-permute-start.17 = (bf16[32,3072]{1,0:T(8,128)(2,1)S(1)}, bf16[32,3072]{1,0:T(8,128)(2,1)S(1)}, u32[]{:S(2)}, u32[]{:S(2)}) collective-permute-start(bf16[32,3072]{1,0:T(8,128)(2,1)S(1)} %collective-permute-done.13.refs_12_), channel_id=1, source_target_pairs={{0,1},{1,0},{2,3},{3,2},{4,5},{5,4},{6,7},{7,6},{8,9},{9,8},{10,11... | collective-permute-start | bytes 589832 | tf_op jit(solution)/shard_map/ppermute | solution.py:311
  81.0 8.9 %collective-permute-start.16 = (bf16[32,3072]{1,0:T(8,128)(2,1)S(1)}, bf16[32,3072]{1,0:T(8,128)(2,1)S(1)}, u32[]{:S(2)}, u32[]{:S(2)}) collective-permute-start(bf16[32,3072]{1,0:T(8,128)(2,1)S(1)} %collective-permute-done.12.refs_11_), channel_id=1, source_target_pairs={{0,1},{1,0},{2,3},{3,2},{4,5},{5,4},{6,7},{7,6},{8,9},{9,8},{10,11... | collective-permute-start | bytes 589832 | tf_op jit(solution)/shard_map/ppermute | solution.py:311
  81.9 8.0 %collective-permute-start.11 = (bf16[32,3072]{1,0:T(8,128)(2,1)S(1)}, bf16[32,3072]{1,0:T(8,128)(2,1)S(1)}, u32[]{:S(2)}, u32[]{:S(2)}) collective-permute-start(bf16[32,3072]{1,0:T(8,128)(2,1)S(1)} %collective-permute-done.7.refs_5_), channel_id=1, source_target_pairs={{0,1},{1,0},{2,3},{3,2},{4,5},{5,4},{6,7},{7,6},{8,9},{9,8},{10,11... | collective-permute-start | bytes 589832 | tf_op jit(solution)/shard_map/ppermute | solution.py:311
  82.0 8.0 %collective-permute-start.18 = (bf16[32,3072]{1,0:T(8,128)(2,1)S(1)}, bf16[32,3072]{1,0:T(8,128)(2,1)S(1)}, u32[]{:S(2)}, u32[]{:S(2)}) collective-permute-start(bf16[32,3072]{1,0:T(8,128)(2,1)S(1)} %collective-permute-done.14.refs_13_), channel_id=1, source_target_pairs={{0,1},{1,0},{2,3},{3,2},{4,5},{5,4},{6,7},{7,6},{8,9},{9,8},{10,11... | collective-permute-start | bytes 589832 | tf_op jit(solution)/shard_map/ppermute | solution.py:311
  89.4 9.6 %collective-permute-start.6 = (bf16[128,768]{1,0:T(8,128)(2,1)}, bf16[128,768]{1,0:T(8,128)(2,1)S(1)}, u32[]{:S(2)}, u32[]{:S(2)}) collective-permute-start(bf16[128,768]{1,0:T(8,128)(2,1)} %bitcast.10), channel_id=1, source_target_pairs={{0,16},{16,0},{1,17},{17,1},{2,18},{18,2},{3,19},{19,3},{4,20},{20... | collective-permute-start | bytes 589832 | tf_op jit(solution)/shard_map/ppermute | solution.py:308
